TPU v7x, 256 devices: a whole 4x4x8 slice. The times are simulated.
256 devices in a mesh: step: 2 (over core), head: 8 (over z), blk: 16 (over y, x).
Axes of the slice: x: 4, y: 4, z: 8, core: 2. Of those that a mesh axis runs over, the one named last changes fastest.
Arguments:
- states: float32 [2, 2048, 3072], P('step', ('head', 'blk')), may hold values from -6 to 6
- start: float32 [2048, 3072], P(('head', 'blk')), may hold values from -6 to 6
- w_qkv: bfloat16 [3072, 3, 3072], P('blk', None, 'head'), may hold values from -0.109375 to 0.109375
- w_out: bfloat16 [3072, 3072], P(('head', 'blk')), may hold values from -0.109375 to 0.109375
- q_gain: float32 [64], replicated, may hold values from 1.5 to 5
- k_gain: float32 [64], replicated, may hold values from 1.5 to 5
- mod_table: float32 [50, 9216], replicated, may hold values from -3 to 3
- step_index: int32 [2], P('step'), may hold values from 0 to 49
- coef_table: float32 [50], replicated, may hold values from 0.1 to 1
- coef_index: int32 [2], P('step'), may hold values from 0 to 49
Outputs:
- new_states: float32 [2, 2048, 3072], P('step', ('head', 'blk'))
All inputs are finite; a program needn't handle non-finite values.
Results may differ from a plain program's by a relative error of at most 0.008.
Values may be sent and summed in bfloat16 or wider, within the bound.
No kernel may reach another device: no remote copies, remote signals or barrier semaphores. Data moves between devices by JAX's collectives and lax.ppermute only.
A program may use at most 128 MiB of HBM per device.

v0:
```python
import jax
import jax.numpy as jnp
from jax import lax
from jax.sharding import PartitionSpec as P

HD = 64


def carried_in(array, axis, join, neutral):
    place = lax.axis_index(axis)
    gathered = lax.all_gather(array.astype(jnp.bfloat16), axis)
    state = jnp.zeros_like(array) + jnp.asarray(neutral, array.dtype)

    def one(step, state):
        return join(state, lax.dynamic_index_in_dim(gathered, step, 0, False).astype(array.dtype))

    return lax.fori_loop(0, place, one, state)


def head_norm(values_in, gains):
    middle = jnp.mean(values_in, axis=-1, keepdims=True)
    spread = jnp.mean((values_in - middle) ** 2, axis=-1, keepdims=True)
    return (values_in - middle) * lax.rsqrt(spread + 1e-06) * gains


def on_device(
    states, start, w_qkv, w_out, q_gain, k_gain, mod_table, step_index, coef_table, coef_index
):
    width = states.shape[2]
    table_size = mod_table.shape[0]
    slot_ids = jnp.arange(table_size, dtype=jnp.int32)[None, :]
    mod_picks = (step_index[:, None] == slot_ids).astype(jnp.float32)
    coef_picks = (coef_index[:, None] == slot_ids).astype(jnp.float32)
    modulation = jnp.dot(mod_picks, mod_table, precision=lax.Precision.HIGHEST).reshape(
        -1, 3, width
    )
    coefs = jnp.sum(coef_picks * coef_table[None, :], axis=1)
    middle = jnp.mean(states, axis=-1, keepdims=True)
    spread = jnp.mean((states - middle) ** 2, axis=-1, keepdims=True)
    normed = (
        (states - middle) * lax.rsqrt(spread + 1e-05) * (1.0 + modulation[:, 1][:, None, :])
        + modulation[:, 0][:, None, :]
    ).astype(jnp.bfloat16)
    weight_rows = lax.all_gather(w_qkv, "blk", axis=0, tiled=True)
    projected = jnp.einsum(
        "std,dce->stce",
        lax.all_gather(normed, "head", axis=1, tiled=True),
        weight_rows,
        preferred_element_type=jnp.float32,
    )
    step_count = projected.shape[0]
    row_count = projected.shape[1]
    local_heads = projected.shape[3] // HD
    queries = head_norm(
        projected[:, :, 0].reshape(step_count, row_count, local_heads, HD), q_gain
    ).astype(jnp.bfloat16)
    keys_here = head_norm(
        projected[:, :, 1].reshape(step_count, row_count, local_heads, HD), k_gain
    ).astype(jnp.bfloat16)
    values_here = (
        projected[:, :, 2].reshape(step_count, row_count, local_heads, HD).astype(jnp.bfloat16)
    )
    scale_factor = HD ** (-0.5)
    start_best = jnp.full((step_count, local_heads, row_count), -1e30, jnp.float32)
    start_totals = jnp.zeros((step_count, local_heads, row_count), jnp.float32)
    start_accum = jnp.zeros((step_count, local_heads, row_count, HD), jnp.float32)
    best = start_best
    totals = start_totals
    accum = start_accum
    key_piece = lax.all_gather(keys_here, "blk", axis=1, tiled=True)
    value_piece = lax.all_gather(values_here, "blk", axis=1, tiled=True)
    length = key_piece.shape[1]
    for offset in range(0, length, 512):
        stop = min(offset + 512, length)
        key_block = key_piece[:, offset:stop]
        value_block = value_piece[:, offset:stop]
        scores = (
            jnp.einsum("sqhd,skhd->shqk", queries, key_block, preferred_element_type=jnp.float32)
            * scale_factor
        )
        new_best = jnp.maximum(best, jnp.max(scores, axis=-1))
        factor = jnp.exp(best - new_best)
        weights = jnp.exp(scores - new_best[..., None])
        totals = totals * factor + jnp.sum(weights, axis=-1)
        accum = accum * factor[..., None] + jnp.einsum(
            "shqk,skhd->shqd",
            weights.astype(jnp.bfloat16),
            value_block,
            preferred_element_type=jnp.float32,
        )
        best = new_best
    best, totals, accum = (best, totals, accum)
    attn = jnp.transpose(accum / totals[..., None], (0, 2, 1, 3)).reshape(
        step_count, row_count, local_heads * HD
    )
    attn = attn.astype(jnp.bfloat16)
    group_terms = jnp.einsum(
        "srf,fe->sre",
        attn,
        lax.all_gather(w_out, "blk", axis=0, tiled=True),
        preferred_element_type=jnp.float32,
    )
    mixed = lax.psum_scatter(
        group_terms.astype(jnp.bfloat16), "head", scatter_dimension=1, tiled=True
    ).astype(jnp.float32)
    drift = modulation[:, 2][:, None, :] * mixed
    inclusive = jnp.cumsum(coefs[:, None, None] * drift, axis=0)
    own_total = inclusive[-1]
    earlier = carried_in(
        own_total, "step", lambda first, second: first + second, jnp.zeros_like(own_total)
    )
    return start[None] + (earlier[None] + inclusive)


def solution(mesh):
    in_specs = (
        P("step", ("head", "blk"), None),
        P(("head", "blk"), None),
        P("blk", None, "head"),
        P(("head", "blk"), None),
        P(),
        P(),
        P(),
        P("step"),
        P(),
        P("step"),
    )
    out_specs = P("step", ("head", "blk"), None)
    return jax.shard_map(
        on_device, mesh=mesh, in_specs=in_specs, out_specs=out_specs, check_vma=False
    )
```

profile of v0, /device:TPU:1, one launch (start us, length us, event | category | flops | bytes accessed | tf_op | source)
XLA Modules:
  0.0 296.6 jit_solution(17532198144011052119)
XLA Ops:
  6.5 0.7 all-gather.5.cloned.1.call-update
  7.3 3.2 %reshape.440 = f32[3,3072,50]{1,0,2:T(4,128)S(1)} reshape(f32[9216,50]{0,1:T(8,128)} %bitcast.98) | data formatting | bytes 3686400 | tf_op jit(solution)/shard_map/reshape.224
  11.3 0.2 multiply_reduce_fusion.2
  11.5 1.8 fusion.1
  13.5 25.1 %all_gather.19 = bf16[1,128,3072]{2,1,0:T(8,128)(2,1)S(1)} all-gather(bf16[1,16,3072]{2,1,0:T(8,128)(2,1)S(1)} %add_convert_fusion), channel_id=1, replica_groups=mesh['step'=2,'head'=8,'blk'=16] {'head'}, dimensions={1}, use_global_device_ids=true | all-gather | bytes 884736 | tf_op jit(solution)/shard_map/all_gather | solution.py:47
  38.6 45.0 %all-gather.5.cloned.1.call-done = bf16[3072,3,384]{2,0,1:T(8,128)(2,1)} async-done(((bf16[192,3,384]{2,0,1:T(8,128)(2,1)}), bf16[3072,3,384]{2,0,1:T(8,128)(2,1)}) %all-gather.5.cloned.1.call-update) | async-done | bytes 7077904 | tf_op jit(solution)/shard_map/all_gather | solution.py:44
  83.5 4.2 %convolution_bitcast_fusion = f32[1,128,3,384]{3,1,2,0:T(8,128)S(1)} fusion(bf16[3072,3,384]{2,0,1:T(8,128)(2,1)} %all-gather.5.cloned.1.call-done, bf16[1,128,3072]{2,1,0:T(8,128)(2,1)S(1)} %all_gather.19), kind=kOutput, calls=%fused_computation.21 | convolution fusion | flops 905969664 | bytes 8454144 | tf_op jit(solution)/shard_map/std,dce->stce/dot_general | solution.py:45
  88.0 0.4 copy-done.8
  88.4 0.7 multiply_convert_fusion
  89.2 0.7 copy.24
  90.0 0.5 all-gather.11.cloned.1.call-update
  90.9 47.2 %all-gather.7.cloned.1.call-done = bf16[1,2048,6,64]{1,3,2,0:T(8,128)(2,1)} async-done(((bf16[1,128,6,64]{1,3,2,0:T(8,128)(2,1)}), bf16[1,2048,6,64]{1,3,2,0:T(8,128)(2,1)}) %all-gather.7.cloned.1.call-update) | async-done | bytes 1572880 | tf_op jit(solution)/shard_map/all_gather | solution.py:70
  138.2 1.6 fusion.41
  139.8 0.5 fusion.40
  140.3 0.5 fusion.39
  140.8 0.5 fusion.38
  141.3 0.9 fusion.3
  142.2 0.2 copy-done.1
  142.5 0.9 fusion.7
  143.4 47.1 %all-gather.9.cloned.1.call-done = bf16[1,2048,6,64]{1,3,2,0:T(8,128)(2,1)} async-done(((bf16[1,128,6,64]{1,3,2,0:T(8,128)(2,1)}), bf16[1,2048,6,64]{1,3,2,0:T(8,128)(2,1)}) %all-gather.9.cloned.1.call-update) | async-done | bytes 1572880 | tf_op jit(solution)/shard_map/all_gather | solution.py:71
  190.5 2.1 fusion.14
  192.5 0.5 fusion.13
  193.0 0.5 fusion.12
  193.5 0.9 copy-done.2
  194.4 0.5 fusion.15
  194.9 48.3 %all-gather.11.cloned.1.call-done = bf16[384,3072]{1,0:T(8,128)(2,1)} async-done(((bf16[24,3072]{1,0:T(8,128)(2,1)}), bf16[384,3072]{1,0:T(8,128)(2,1)}) %all-gather.11.cloned.1.call-update) | async-done | bytes 2359312 | tf_op jit(solution)/shard_map/all_gather | solution.py:100
  243.3 3.2 %fusion = bf16[1,128,3072]{2,1,0:T(8,128)(2,1)} fusion(bf16[128,384]{0,1:T(8,128)(2,1)S(1)} %bitcast.102, bf16[384,3072]{1,0:T(8,128)(2,1)} %all-gather.11.cloned.1.call-done), kind=kOutput, calls=%fused_computation.2 | convolution fusion | flops 302383104 | bytes 3244032 | tf_op jit(solution)/shard_map/srf,fe->sre/dot_general | solution.py:97
  247.1 0.6 fusion.30
  247.7 32.7 %reduce-scatter.2.cloned.1.call-done = bf16[1,16,3072]{2,1,0:T(8,128)(2,1)} async-done(((bf16[1,128,3072]{2,1,0:T(8,128)(2,1)}), bf16[1,16,3072]{2,1,0:T(8,128)(2,1)}) %reduce-scatter.2.cloned.1.call-update) | async-done | bytes 98320 | tf_op jit(solution)/shard_map/reduce_scatter | solution.py:103
  280.4 1.5 fusion.26
  281.9 6.8 %all_gather.24 = bf16[2,16,3072]{2,1,0:T(8,128)(2,1)S(1)} all-gather(bf16[1,16,3072]{2,1,0:T(8,128)(2,1)S(1)} %fusion.26), channel_id=1, replica_groups=mesh['step'=2,'head'=8,'blk'=16] {'step'}, dimensions={0}, use_global_device_ids=true | all-gather | bytes 294912 | tf_op jit(solution)/shard_map/all_gather | solution.py:11
  288.8 1.3 fusion.25
  (51 shorter events, 1.2 us)
Async XLA Ops:
  6.5 77.0 %all-gather.5.cloned.1.call-start = ((), (), s32[]{:S(2)}) async-start(), calls=%async_computation.1 | async-start | bytes 7520256 | tf_op jit(solution)/shard_map/all_gather | solution.py:44
  7.3 130.9 %all-gather.7.cloned.1.call-start = ((), (), s32[]{:S(2)}) async-start(), calls=%async_computation.2 | async-start | bytes 1671168 | tf_op jit(solution)/shard_map/all_gather | solution.py:70
  7.3 3.8 %copy-start.3 = (f32[1,16,3072]{2,1,0:T(8,128)S(1)}, f32[1,16,3072]{2,1,0:T(8,128)}, u32[]{:S(2)}) copy-start(f32[1,16,3072]{2,1,0:T(8,128)} %param.12) | copy-start | bytes 589828
  87.8 0.7 copy-start.8
  87.8 3.1 %copy-start.9 = (f32[64]{0:T(128)S(1)}, f32[64]{0:T(128)}, u32[]{:S(2)}) copy-start(f32[64]{0:T(128)} %param.16) | copy-start | bytes 772
  89.2 101.3 %all-gather.9.cloned.1.call-start = ((), (), s32[]{:S(2)}) async-start(), calls=%async_computation.3 | async-start | bytes 1671168 | tf_op jit(solution)/shard_map/all_gather | solution.py:71
  90.0 153.3 %all-gather.11.cloned.1.call-start = ((), (), s32[]{:S(2)}) async-start(), calls=%async_computation.4 | async-start | bytes 2506752 | tf_op jit(solution)/shard_map/all_gather | solution.py:100
  90.6 189.8 %reduce-scatter.2.cloned.1.call-start = ((), (), s32[]{:S(2)}) async-start(), calls=%async_computation.5 | async-start | bytes 884736 | tf_op jit(solution)/shard_map/reduce_scatter | solution.py:103
  138.2 1.6 copy-start.4
  139.8 1.5 copy-start
  141.3 1.2 copy-start.1
  190.5 2.1 copy-start.5
  193.0 1.4 copy-start.2
  243.3 3.9 %copy-start.10 = (f32[50]{0:T(128)S(1)}, f32[50]{0:T(128)}, u32[]{:S(2)}) copy-start(f32[50]{0:T(128)} %param.20) | copy-start | bytes 604
  281.9 6.9 %copy-start.6 = (bf16[1,16,3072]{2,1,0:T(8,128)(2,1)S(1)}, bf16[1,16,3072]{2,1,0:T(8,128)(2,1)}, u32[]{:S(2)}) copy-start(bf16[1,16,3072]{2,1,0:T(8,128)(2,1)} %reduce-scatter.2.cloned.1.call-done) | copy-start | bytes 294916
  281.9 6.9 %copy-start.7 = (f32[16,3072]{1,0:T(8,128)S(1)}, f32[16,3072]{1,0:T(8,128)}, u32[]{:S(2)}) copy-start(f32[16,3072]{1,0:T(8,128)} %param.13) | copy-start | bytes 589828
Sparse Core Ops, SparseCore 0:
  9.8 73.7 all-gather.4
  89.3 48.8 all-gather.6
  140.6 49.8 all-gather.8
  192.8 50.4 all-gather.10
  246.6 33.7 reduce-scatter.1
where the time goes:
time: 297 us
  waiting for transfers between devices  222 us (75%)
  blocking collectives  31.8 us (11%)
  matrix products  15.8 us (5%)
  between operations  14.8 us (5%)
  other arithmetic  6.61 us (2%)
  local copies, waits for them, and re-layouts  5.77 us (2%)
    all_gather x1, waiting for transfers between devices, on_device(): lax.all_gather(w_out, 'blk', axis=0, tiled=True)  48.3 us
    all_gather x1, waiting for transfers between devices, on_device(): key_piece = lax.all_gather(keys_here, 'blk', axis=1, tiled=True)  47.2 us
    all_gather x1, waiting for transfers between devices, on_device(): value_piece = lax.all_gather(values_here, 'blk', axis=1, tiled=True)  47.1 us
    all_gather x1, waiting for transfers between devices, on_device(): weight_rows = lax.all_gather(w_qkv, 'blk', axis=0, tiled=True)  45 us
    reduce_scatter x1, waiting for transfers between devices, on_device(): lax.psum_scatter(group_terms.astype(jnp.bfloat16), 'head', scatter_dimens...  32.7 us
    all_gather x1, blocking collectives, on_device(): lax.all_gather(normed, 'head', axis=1, tiled=True)  25.1 us
    all_gather x1, blocking collectives, carried_in(): gathered = lax.all_gather(array.astype(jnp.bfloat16), axis)  6.76 us
  transfers between devices with their start and end apart: 5, of which 5 were waited for; matrix products, arithmetic and copies ran while one was open for 5% of the time, Pallas kernels for 0%

commit v1 on v0

--- a/solution.py
+++ b/solution.py
@@ -41,7 +41,9 @@
         (states - middle) * lax.rsqrt(spread + 1e-05) * (1.0 + modulation[:, 1][:, None, :])
         + modulation[:, 0][:, None, :]
     ).astype(jnp.bfloat16)
-    weight_rows = lax.all_gather(w_qkv, "blk", axis=0, tiled=True)
+    weight_rows = jnp.concatenate(
+        lax.all_to_all(jnp.stack([w_qkv] * lax.axis_size("blk")), "blk", 0, 0), axis=0
+    )
     projected = jnp.einsum(
         "std,dce->stce",
         lax.all_gather(normed, "head", axis=1, tiled=True),

time: 297 us -> 341 us (1.15)
  waiting for transfers between devices: 222 us -> 249 us
  local copies, waits for them, and re-layouts: 5.77 us -> 14.7 us
  starting transfers between devices: 0.16 us -> 7.79 us
    all_to_all x0 -> x1, waiting for transfers between devices: none -> 71.2 us  [on_device(): lax.all_to_all(jnp.stack([w_qkv] * lax.axis_size('blk')), 'blk', 0, 0)]
    all_gather x1 -> x0, waiting for transfers between devices: 45 us -> none  [on_device(): weight_rows = lax.all_gather(w_qkv, 'blk', axis=0, tiled=True)]
    all_to_all x0 -> x1, starting transfers between devices: none -> 7.63 us  [on_device(): lax.all_to_all(jnp.stack([w_qkv] * lax.axis_size('blk')), 'blk', 0, 0)]
    another operation x1 -> x2, local copies, waits for them, and re-layouts: 3.17 us -> 8.24 us  [the longest x1 5.07 us: on_device(): jnp.stack([w_qkv] * lax.axis_size('blk'))]
    all_to_all x0 -> x1, local copies, waits for them, and re-layouts: none -> 3.88 us  [on_device(): lax.all_to_all(jnp.stack([w_qkv] * lax.axis_size('blk')), 'blk', 0, 0)]
where the time goes in v1:
time: 341 us; the launch traced here: 340 us
  waiting for transfers between devices  249 us (73%)
  blocking collectives  33.6 us (10%)
  between operations  14.8 us (4%)
  local copies, waits for them, and re-layouts  14.7 us (4%)
  matrix products  13.4 us (4%)
  starting transfers between devices  7.79 us (2%)
  other arithmetic  6.95 us (2%)
    all_to_all x1, waiting for transfers between devices, on_device(): lax.all_to_all(jnp.stack([w_qkv] * lax.axis_size('blk')), 'blk', 0, 0)  71.2 us
    all_gather x1, waiting for transfers between devices, on_device(): key_piece = lax.all_gather(keys_here, 'blk', axis=1, tiled=True)  50.1 us
    all_gather x1, waiting for transfers between devices, on_device(): lax.all_gather(w_out, 'blk', axis=0, tiled=True)  47.9 us
    all_gather x1, waiting for transfers between devices, on_device(): value_piece = lax.all_gather(values_here, 'blk', axis=1, tiled=True)  47.1 us
    reduce_scatter x1, waiting for transfers between devices, on_device(): lax.psum_scatter(group_terms.astype(jnp.bfloat16), 'head', scatter_dimens...  32.2 us
    all_gather x1, blocking collectives, on_device(): lax.all_gather(normed, 'head', axis=1, tiled=True)  26.5 us
    all_to_all x1, starting transfers between devices, on_device(): lax.all_to_all(jnp.stack([w_qkv] * lax.axis_size('blk')), 'blk', 0, 0)  7.63 us
    all_gather x1, blocking collectives, carried_in(): gathered = lax.all_gather(array.astype(jnp.bfloat16), axis)  7.15 us
  transfers between devices with their start and end apart: 5, of which 5 were waited for; matrix products, arithmetic and copies ran while one was open for 5% of the time, Pallas kernels for 0%

profile of v1, /device:TPU:1, one launch (start us, length us, event | category | flops | bytes accessed | tf_op | source)
XLA Modules:
  0.0 340.4 jit_solution(16684380612365796021)
XLA Ops:
  6.5 5.1 %stack.2 = bf16[16,192,3,384]{3,1,2,0:T(8,128)(2,1)} broadcast(bf16[192,3,384]{2,0,1:T(8,128)(2,1)} %param.14), dimensions={1,2,3} | broadcast | bytes 7520256 | tf_op jit(solution)/shard_map/stack | solution.py:45
  11.6 7.6 %all-to-all-start = ((bf16[16,192,3,384]{3,1,2,0:T(8,128)(2,1)}), bf16[16,192,3,384]{3,1,2,0:T(8,128)(2,1)}, u32[]{:S(2)}, u32[]{:S(2)}) async-start(bf16[16,192,3,384]{3,1,2,0:T(8,128)(2,1)} %stack.2), calls=%async_computation | async-start | bytes 14155776 | tf_op jit(solution)/shard_map/all_to_all | solution.py:45
  19.3 3.2 reshape.445
  23.5 1.8 fusion.1
  25.5 26.5 %all_gather.16 = bf16[1,128,3072]{2,1,0:T(8,128)(2,1)S(1)} all-gather(bf16[1,16,3072]{2,1,0:T(8,128)(2,1)S(1)} %add_convert_fusion), channel_id=1, replica_groups=mesh['step'=2,'head'=8,'blk'=16] {'head'}, dimensions={1}, use_global_device_ids=true | all-gather | bytes 884736 | tf_op jit(solution)/shard_map/all_gather | solution.py:49
  51.9 71.2 %all-to-all-done = bf16[16,192,3,384]{3,1,2,0:T(8,128)(2,1)} async-done(((bf16[16,192,3,384]{3,1,2,0:T(8,128)(2,1)}), bf16[16,192,3,384]{3,1,2,0:T(8,128)(2,1)}, u32[]{:S(2)}, u32[]{:S(2)}) %all-to-all-start) | async-done | bytes 7077920 | tf_op jit(solution)/shard_map/all_to_all | solution.py:45
  123.1 3.9 %copy.20 = bf16[16,192,3,384]{3,1,0,2:T(8,128)(2,1)S(1)} copy(bf16[16,192,3,384]{3,1,2,0:T(8,128)(2,1)} %all-to-all-done) | data formatting | bytes 14155776 | tf_op jit(solution)/shard_map/all_to_all | solution.py:45
  127.0 1.2 convolution_bitcast_fusion
  128.5 0.4 copy-done.9
  128.9 0.7 multiply_convert_fusion
  129.7 0.7 copy.25
  130.5 0.7 all-gather.8.cloned.1.call-update
  131.6 50.1 %all-gather.4.cloned.1.call-done = bf16[1,2048,6,64]{1,3,2,0:T(8,128)(2,1)} async-done(((bf16[1,128,6,64]{1,3,2,0:T(8,128)(2,1)}), bf16[1,2048,6,64]{1,3,2,0:T(8,128)(2,1)}) %all-gather.4.cloned.1.call-update) | async-done | bytes 1572880 | tf_op jit(solution)/shard_map/all_gather | solution.py:72
  181.7 1.6 fusion.41
  183.3 0.5 fusion.38
  183.8 0.5 fusion.39
  184.3 0.5 fusion.40
  184.9 0.9 fusion.7
  185.9 0.9 fusion.3
  186.9 47.1 %all-gather.6.cloned.1.call-done = bf16[1,2048,6,64]{1,3,2,0:T(8,128)(2,1)} async-done(((bf16[1,128,6,64]{1,3,2,0:T(8,128)(2,1)}), bf16[1,2048,6,64]{1,3,2,0:T(8,128)(2,1)}) %all-gather.6.cloned.1.call-update) | async-done | bytes 1572880 | tf_op jit(solution)/shard_map/all_gather | solution.py:73
  233.9 1.6 fusion.14
  235.5 1.6 fusion.13
  237.1 0.5 fusion.12
  237.6 0.9 copy-done.3
  238.5 0.5 fusion.15
  239.0 47.9 %all-gather.8.cloned.1.call-done = bf16[384,3072]{1,0:T(8,128)(2,1)} async-done(((bf16[24,3072]{1,0:T(8,128)(2,1)}), bf16[384,3072]{1,0:T(8,128)(2,1)}) %all-gather.8.cloned.1.call-update) | async-done | bytes 2359312 | tf_op jit(solution)/shard_map/all_gather | solution.py:102
  286.9 3.2 fusion
  290.7 0.7 fusion.30
  291.4 32.2 %reduce-scatter.2.cloned.1.call-done = bf16[1,16,3072]{2,1,0:T(8,128)(2,1)} async-done(((bf16[1,128,3072]{2,1,0:T(8,128)(2,1)}), bf16[1,16,3072]{2,1,0:T(8,128)(2,1)}) %reduce-scatter.2.cloned.1.call-update) | async-done | bytes 98320 | tf_op jit(solution)/shard_map/reduce_scatter | solution.py:105
  323.6 1.6 fusion.26
  325.2 7.2 %all_gather.20 = bf16[2,16,3072]{2,1,0:T(8,128)(2,1)S(1)} all-gather(bf16[1,16,3072]{2,1,0:T(8,128)(2,1)S(1)} %fusion.26), channel_id=1, replica_groups=mesh['step'=2,'head'=8,'blk'=16] {'step'}, dimensions={0}, use_global_device_ids=true | all-gather | bytes 294912 | tf_op jit(solution)/shard_map/all_gather | solution.py:11
  332.5 1.4 fusion.25
  (54 shorter events, 1.7 us)
Async XLA Ops:
  11.6 111.5 %all-to-all-start = ((bf16[16,192,3,384]{3,1,2,0:T(8,128)(2,1)}), bf16[16,192,3,384]{3,1,2,0:T(8,128)(2,1)}, u32[]{:S(2)}, u32[]{:S(2)}) async-start(bf16[16,192,3,384]{3,1,2,0:T(8,128)(2,1)} %stack.2), calls=%async_computation | async-start | bytes 14155776 | tf_op jit(solution)/shard_map/all_to_all | solution.py:45
  19.2 162.4 %all-gather.4.cloned.1.call-start = ((), (), s32[]{:S(2)}) async-start(), calls=%async_computation.2 | async-start | bytes 1671168 | tf_op jit(solution)/shard_map/all_gather | solution.py:72
  19.3 3.8 %copy-start.4 = (f32[1,16,3072]{2,1,0:T(8,128)S(1)}, f32[1,16,3072]{2,1,0:T(8,128)}, u32[]{:S(2)}) copy-start(f32[1,16,3072]{2,1,0:T(8,128)} %param.12) | copy-start | bytes 589828
  128.2 0.7 copy-start.9
  128.2 3.2 copy-start.10
  129.6 104.3 %all-gather.6.cloned.1.call-start = ((), (), s32[]{:S(2)}) async-start(), calls=%async_computation.3 | async-start | bytes 1671168 | tf_op jit(solution)/shard_map/all_gather | solution.py:73
  130.5 156.4 %all-gather.8.cloned.1.call-start = ((), (), s32[]{:S(2)}) async-start(), calls=%async_computation.4 | async-start | bytes 2506752 | tf_op jit(solution)/shard_map/all_gather | solution.py:102
  131.2 192.4 %reduce-scatter.2.cloned.1.call-start = ((), (), s32[]{:S(2)}) async-start(), calls=%async_computation.5 | async-start | bytes 884736 | tf_op jit(solution)/shard_map/reduce_scatter | solution.py:105
  181.7 1.6 copy-start.5
  183.8 1.2 copy-start.2
  184.8 1.2 copy-start
  233.9 1.6 copy-start.1
  235.5 1.6 copy-start.6
  237.1 1.4 copy-start.3
  286.9 3.9 %copy-start.11 = (f32[50]{0:T(128)S(1)}, f32[50]{0:T(128)}, u32[]{:S(2)}) copy-start(f32[50]{0:T(128)} %param.20) | copy-start | bytes 604
  325.2 7.3 %copy-start.7 = (bf16[1,16,3072]{2,1,0:T(8,128)(2,1)S(1)}, bf16[1,16,3072]{2,1,0:T(8,128)(2,1)}, u32[]{:S(2)}) copy-start(bf16[1,16,3072]{2,1,0:T(8,128)(2,1)} %reduce-scatter.2.cloned.1.call-done) | copy-start | bytes 294916
  325.2 7.3 %copy-start.8 = (f32[16,3072]{1,0:T(8,128)S(1)}, f32[16,3072]{1,0:T(8,128)}, u32[]{:S(2)}) copy-start(f32[16,3072]{1,0:T(8,128)} %param.13) | copy-start | bytes 589828
Sparse Core Ops, SparseCore 0:
  129.7 51.8 all-gather.3
  184.1 49.8 all-gather.5
  236.4 50.4 all-gather.7
  290.2 33.3 reduce-scatter.1
